TPU v7x, 32 devices: a whole 2x2x4 slice. The times are simulated.
32 devices in a mesh: row: 8 (over y, x, core), col: 4 (over z).
Axes of the slice: x: 2, y: 2, z: 4, core: 2. Of those that a mesh axis runs over, the one named last changes fastest.
Arguments:
- covariance: float32 [2, 8, 512, 4, 4, 512], P(None, 'row', None, None, 'col'), as said below
- keep: int32 [2, 8, 4, 4], P(None, 'row', None, 'col'), may hold values from 0 to 1, as said below
Outputs:
- factor: float32 [2, 8, 512, 4, 4, 512], P(None, 'row', None, None, 'col')
Inputs may be any that keep to these rules, and one draw needn't show every extreme that they name: covariance is symmetric and positive definite. keep is 1 for every tile pair whose row and column tiles lie in the same diagonal super-tile of 4 tiles (i // 4 == j // 4).
All inputs are finite; a program needn't handle non-finite values.
Results may differ from a plain program's by a relative error of at most 0.0001.
Values sent between devices are 32-bit elements; how exact they have to be, the bound alone decides.
A program may use at most 128 MiB of HBM per device.

v0:
```python
import jax
import jax.numpy as jnp
from jax import lax
from jax.sharding import PartitionSpec as P

HIGH = lax.Precision.HIGHEST


def from_root(block, axis, source):
    block = jnp.where(lax.axis_index(axis) == source, block, jnp.zeros_like(block))
    return lax.psum(block, axis)


def mm(a, b):
    return jnp.matmul(a, b, precision=HIGH)


def factor_block(block):
    lower = jnp.linalg.cholesky(block)
    eye = jnp.eye(block.shape[0], dtype=jnp.float32)
    return (lower, lax.linalg.triangular_solve(lower, eye, left_side=True, lower=True))


def factor_and_inverse(block):
    width = block.shape[0]
    if width <= 128:
        return factor_block(block)
    half = width // 2
    l00, i00 = factor_and_inverse(block[:half, :half])
    l10 = mm(block[half:, :half], i00.T)
    l11, i11 = factor_and_inverse(block[half:, half:] - mm(l10, l10.T))
    i10 = -mm(i11, mm(l10, i00))
    zero = jnp.zeros((half, half), jnp.float32)
    return (jnp.block([[l00, zero], [l10, l11]]), jnp.block([[i00, zero], [i10, i11]]))


def finish(solved, factor, ids, step):
    return jnp.where(
        ids[:, None, None] > step,
        solved,
        jnp.where(ids[:, None, None] == step, factor[None], jnp.float32(0.0)),
    )


def shards(covariance, keep):
    row_count = lax.axis_size("row")
    col_count = lax.axis_size("col")
    row_here = lax.axis_index("row")
    col_here = lax.axis_index("col")
    tile_rows = covariance.shape[0]
    width = covariance.shape[2]
    tile_cols = covariance.shape[3]
    group = row_count // col_count
    tiles = covariance.reshape(tile_rows, width, tile_cols, width)
    row_ids = jnp.arange(tile_rows) * row_count + row_here
    col_ids = jnp.arange(tile_cols) * col_count + col_here
    live = (keep.reshape(tile_rows, tile_cols) > 0) & (row_ids[:, None] >= col_ids[None, :])
    tiles = jnp.where(live[:, None, :, None], tiles, jnp.float32(0.0))

    def spread_rows(block, step):
        return from_root(block, "col", step % col_count)

    def column_tiles(block):
        received = []
        for member in range(group):
            received.append(from_root(block, "row", col_here + member * col_count))
        stacked = jnp.stack(received, 1)
        return stacked.reshape(tile_rows * group, width, width)

    def factor_panel(column_block, step):
        local_diag = column_block[step // row_count]
        diag_tile = from_root(local_diag, "row", step % row_count)
        on_column = col_here == step % col_count
        factor, inverse = factor_and_inverse((diag_tile + diag_tile.T) * 0.5)
        row_panel = finish(mm(column_block, inverse.T), factor, row_ids, step)
        row_panel = jnp.where(on_column, row_panel, jnp.float32(0.0))
        row_panel = spread_rows(row_panel, step)
        col_panel = column_tiles(row_panel)
        return (row_panel, col_panel)

    def apply_update(block, row_panel, col_panel, step):
        product = jnp.einsum("arb,csb->arcs", row_panel, col_panel, precision=lax.Precision.HIGHEST)
        active = live & (row_ids > step)[:, None] & (col_ids > step)[None, :]
        updated = jnp.where(active[:, None, :, None], block - product, block)
        return jnp.where((col_ids == step)[None, None, :, None], row_panel[:, :, None, :], updated)

    first_rows, first_cols = factor_panel(tiles[:, :, 0, :], 0)
    tiles = apply_update(tiles, first_rows, first_cols, 0)
    second_rows, second_cols = factor_panel(tiles[:, :, 0, :], 1)
    tiles = apply_update(tiles, second_rows, second_cols, 1)
    return tiles.reshape(tile_rows, 1, width, tile_cols, 1, width)


def solution(mesh):
    placed = (P(None, "row", None, None, "col", None), P(None, "row", None, "col"))
    return jax.shard_map(
        shards,
        mesh=mesh,
        in_specs=placed,
        out_specs=P(None, "row", None, None, "col", None),
        check_vma=False,
    )
```

profile of v0, /device:TPU:0, one launch (start us, length us, event | category | flops | bytes accessed | tf_op | source)
XLA Modules:
  0.0 754.2 jit_solution(4689376273525011006)
XLA Ops:
  6.6 0.8 and_and_fusion
  7.3 6.1 bitcast_select_fusion
  13.5 3.4 copy-done
  16.9 1.1 fusion.18
  18.3 59.2 %all-reduce.21.cloned.1.call-done = f32[512,512]{1,0:T(8,128)} async-done(((f32[512,512]{1,0:T(8,128)}), f32[512,512]{1,0:T(8,128)}) %all-reduce.21.cloned.1.call-update) | async-done | bytes 1048592 | tf_op jit(solution)/shard_map/psum | solution.py:11
  77.5 1.6 copy.37
  79.5 11.7 %cholesky.134 = f32[128,128]{1,0:T(8,128)S(1)} custom-call(f32[128,128]{1,0:T(8,128)S(1)} %fusion.93), custom_call_target="Cholesky" | custom-call | tf_op jit(solution)/shard_map/jit(cholesky)/cholesky | solution.py:19
  91.2 0.7 compare_reduce_fusion.7
  92.7 9.8 %custom-call.12 = f32[1,128,128]{1,2,0:T(8,128)S(1)} custom-call(f32[1,128,128]{2,1,0:T(8,128)S(1)} %get-tuple-element.27), custom_call_target="InvertDiagBlocksLowerTriangular" | custom-call | tf_op jit(solution)/shard_map/triangular_solve/custom-call.0 | solution.py:21
  103.7 11.7 %cholesky.145 = f32[128,128]{1,0:T(8,128)S(1)} custom-call(f32[128,128]{1,0:T(8,128)S(1)} %fusion.91), custom_call_target="Cholesky" | custom-call | tf_op jit(solution)/shard_map/jit(cholesky)/cholesky | solution.py:19
  116.9 10.0 %custom-call.13 = f32[1,128,128]{1,2,0:T(8,128)S(1)} custom-call(f32[1,128,128]{2,1,0:T(8,128)S(1)} %get-tuple-element.25), custom_call_target="InvertDiagBlocksLowerTriangular" | custom-call | tf_op jit(solution)/shard_map/triangular_solve/custom-call.0 | solution.py:21
  128.7 11.7 %cholesky.156 = f32[128,128]{1,0:T(8,128)S(1)} custom-call(f32[128,128]{1,0:T(8,128)S(1)} %fusion.89), custom_call_target="Cholesky" | custom-call | tf_op jit(solution)/shard_map/jit(cholesky)/cholesky | solution.py:19
  140.4 0.7 compare_reduce_fusion.5
  141.9 9.8 %custom-call.14 = f32[1,128,128]{1,2,0:T(8,128)S(1)} custom-call(f32[1,128,128]{2,1,0:T(8,128)S(1)} %get-tuple-element.23), custom_call_target="InvertDiagBlocksLowerTriangular" | custom-call | tf_op jit(solution)/shard_map/triangular_solve/custom-call.0 | solution.py:21
  153.8 12.1 %cholesky.167 = f32[128,128]{1,0:T(8,128)S(1)} custom-call(f32[128,128]{1,0:T(8,128)S(1)} %fusion.87), custom_call_target="Cholesky" | custom-call | tf_op jit(solution)/shard_map/jit(cholesky)/cholesky | solution.py:19
  166.0 0.7 compare_reduce_fusion.4
  167.4 9.8 %custom-call.15 = f32[1,128,128]{1,2,0:T(8,128)S(1)} custom-call(f32[1,128,128]{2,1,0:T(8,128)S(1)} %get-tuple-element.21), custom_call_target="InvertDiagBlocksLowerTriangular" | custom-call | tf_op jit(solution)/shard_map/triangular_solve/custom-call.0 | solution.py:21
  178.4 6.5 select_select_fusion.1
  185.0 85.7 %all-reduce.23.cloned.1.call-done = f32[2,512,512]{2,1,0:T(8,128)} async-done(((f32[2,512,512]{2,1,0:T(8,128)}), f32[2,512,512]{2,1,0:T(8,128)}) %all-reduce.23.cloned.1.call-update) | async-done | bytes 2097168 | tf_op jit(solution)/shard_map/psum | solution.py:11
  270.7 4.3 select_bitcast_fusion.3
  275.4 80.0 %all-reduce.31.cloned.1.call-done = (f32[2,1,512,512]{3,2,0,1:T(8,128)}, f32[2,1,512,512]{3,2,0,1:T(8,128)}) async-done(((f32[2,1,512,512]{3,2,0,1:T(8,128)}, f32[2,1,512,512]{3,2,0,1:T(8,128)}), (f32[2,1,512,512]{3,2,0,1:T(8,128)}, f32[2,1,512,512]{3,2,0,1:T(8,128)})) %all-reduce.31.cloned.1.call-update) | async-done | bytes 4194320 | tf_op jit(solution)/shard_map/psum | solution.py:11
  355.4 2.8 pad_maximum_fusion
  358.8 1.7 slice-done.1
  361.1 14.2 %fusion = f32[2,512,4,512]{3,1,2,0:T(8,128)S(1)} fusion(f32[2,512,4,512]{3,1,2,0:T(8,128)S(1)} %bitcast.174, f32[2,512,512]{2,1,0:T(8,128)S(1)} %copy-done.2, pred[4]{0:T(512)(128)(4,1)S(1)} %get-tuple-element.36, pred[2,4]{1,0:T(4,128)(4,1)S(1)} %bitcast.179, f32[4,512,512,1]{2,1,0,3:T(8,128)S(1)} %bitcast.177), kind=kOutput, calls=%fused_computation.2 | convolution fusion | flops 12891193344 | bytes 23068684 | tf_op jit(solution)/shard_map/arb,csb->arcs/dot_general | solution.py:82
  375.3 3.4 copy-done.1
  378.7 1.1 fusion.12
  380.0 56.8 %all-reduce.25.cloned.1.call-done = f32[512,512]{1,0:T(8,128)} async-done(((f32[512,512]{1,0:T(8,128)}), f32[512,512]{1,0:T(8,128)}) %all-reduce.25.cloned.1.call-update) | async-done | bytes 1048592 | tf_op jit(solution)/shard_map/psum | solution.py:11
  436.7 1.6 copy.53
  439.2 11.7 %cholesky.178 = f32[128,128]{1,0:T(8,128)S(1)} custom-call(f32[128,128]{1,0:T(8,128)S(1)} %fusion.85), custom_call_target="Cholesky" | custom-call | tf_op jit(solution)/shard_map/jit(cholesky)/cholesky | solution.py:19
  450.9 0.7 compare_reduce_fusion.3
  452.4 9.8 %custom-call.16 = f32[1,128,128]{1,2,0:T(8,128)S(1)} custom-call(f32[1,128,128]{2,1,0:T(8,128)S(1)} %get-tuple-element.19), custom_call_target="InvertDiagBlocksLowerTriangular" | custom-call | tf_op jit(solution)/shard_map/triangular_solve/custom-call.0 | solution.py:21
  463.4 11.7 %cholesky.189 = f32[128,128]{1,0:T(8,128)S(1)} custom-call(f32[128,128]{1,0:T(8,128)S(1)} %fusion.83), custom_call_target="Cholesky" | custom-call | tf_op jit(solution)/shard_map/jit(cholesky)/cholesky | solution.py:19
  475.1 0.7 compare_reduce_fusion.2
  476.6 9.9 %custom-call.17 = f32[1,128,128]{1,2,0:T(8,128)S(1)} custom-call(f32[1,128,128]{2,1,0:T(8,128)S(1)} %get-tuple-element.17), custom_call_target="InvertDiagBlocksLowerTriangular" | custom-call | tf_op jit(solution)/shard_map/triangular_solve/custom-call.0 | solution.py:21
  488.3 11.7 %cholesky.200 = f32[128,128]{1,0:T(8,128)S(1)} custom-call(f32[128,128]{1,0:T(8,128)S(1)} %fusion.81), custom_call_target="Cholesky" | custom-call | tf_op jit(solution)/shard_map/jit(cholesky)/cholesky | solution.py:19
  500.1 0.7 compare_reduce_fusion.1
  501.5 9.8 %custom-call.18 = f32[1,128,128]{1,2,0:T(8,128)S(1)} custom-call(f32[1,128,128]{2,1,0:T(8,128)S(1)} %get-tuple-element.15), custom_call_target="InvertDiagBlocksLowerTriangular" | custom-call | tf_op jit(solution)/shard_map/triangular_solve/custom-call.0 | solution.py:21
  513.5 11.9 %cholesky.211 = f32[128,128]{1,0:T(8,128)S(1)} custom-call(f32[128,128]{1,0:T(8,128)S(1)} %fusion.79), custom_call_target="Cholesky" | custom-call | tf_op jit(solution)/shard_map/jit(cholesky)/cholesky | solution.py:19
  525.4 0.7 compare_reduce_fusion
  526.9 9.8 %custom-call.19 = f32[1,128,128]{1,2,0:T(8,128)S(1)} custom-call(f32[1,128,128]{2,1,0:T(8,128)S(1)} %get-tuple-element.13), custom_call_target="InvertDiagBlocksLowerTriangular" | custom-call | tf_op jit(solution)/shard_map/triangular_solve/custom-call.0 | solution.py:21
  537.9 6.5 select_select_fusion
  544.8 85.3 %all-reduce.27.cloned.1.call-done = f32[2,512,512]{2,1,0:T(8,128)} async-done(((f32[2,512,512]{2,1,0:T(8,128)}), f32[2,512,512]{2,1,0:T(8,128)}) %all-reduce.27.cloned.1.call-update) | async-done | bytes 2097168 | tf_op jit(solution)/shard_map/psum | solution.py:11
  630.1 4.3 select_bitcast_fusion.1
  634.5 80.3 %all-reduce.29.cloned.1.call-done = (f32[2,1,512,512]{3,2,0,1:T(8,128)}, f32[2,1,512,512]{3,2,0,1:T(8,128)}) async-done(((f32[2,1,512,512]{3,2,0,1:T(8,128)}, f32[2,1,512,512]{3,2,0,1:T(8,128)}), (f32[2,1,512,512]{3,2,0,1:T(8,128)}, f32[2,1,512,512]{3,2,0,1:T(8,128)})) %all-reduce.29.cloned.1.call-update) | async-done | bytes 4194320 | tf_op jit(solution)/shard_map/psum | solution.py:11
  714.8 2.8 pad_maximum_fusion.1
  718.2 1.7 slice-done.3
  720.6 14.0 %fusion.2 = f32[2,1,512,4,1,512]{5,2,3,0,4,1:T(8,128)S(1)} fusion(f32[2,512,4,512]{3,1,2,0:T(8,128)S(1)} %bitcast.176, f32[2,512,512]{2,1,0:T(8,128)S(1)} %copy-done.3, pred[4]{0:T(512)(128)(4,1)S(1)} %broadcast_compare_fusion.7, pred[2,4]{1,0:T(4,128)(4,1)S(1)} %bitcast.180, f32[4,512,512,1]{2,1,0,3:T(8,128)S(1)} %bitcast.178), kind=kOutput, calls=%fused_computation.4 | convolution fusion | flops 12891193344 | bytes 23068684 | tf_op jit(solution)/shard_map/arb,csb->arcs/dot_general | solution.py:82
  734.5 12.7 %copy.70 = f32[2,1,512,4,1,512]{5,4,3,2,1,0:T(1,128)} copy(f32[2,1,512,4,1,512]{5,2,3,0,4,1:T(8,128)S(1)} %fusion.2) | data formatting | bytes 16777216 | tf_op jit(solution)/shard_map/reshape | solution.py:91
  (135 shorter events, 23.6 us)
Async XLA Ops:
  6.5 70.9 %all-reduce.21.cloned.1.call-start = ((), (), s32[]{:S(2)}) async-start(), calls=%async_computation | async-start | bytes 2097152 | tf_op jit(solution)/shard_map/psum | solution.py:11
  13.5 3.4 copy-start
  18.0 252.7 %all-reduce.23.cloned.1.call-start = ((), (), s32[]{:S(2)}) async-start(), calls=%async_computation.1 | async-start | bytes 4194304 | tf_op jit(solution)/shard_map/psum | solution.py:11
  77.5 1.7 copy-start.4
  185.0 170.4 %all-reduce.31.cloned.1.call-start = ((), (), s32[]{:S(2)}) async-start(), calls=%async_computation.5 | async-start | bytes 8388608 | tf_op jit(solution)/shard_map/psum | solution.py:11
  275.0 161.7 %all-reduce.25.cloned.1.call-start = ((), (), s32[]{:S(2)}) async-start(), calls=%async_computation.2 | async-start | bytes 2097152 | tf_op jit(solution)/shard_map/psum | solution.py:11
  355.4 3.4 slice-start
  358.2 2.3 slice-start.1
  358.2 2.9 copy-start.2
  375.3 3.4 copy-start.1
  379.9 250.2 %all-reduce.27.cloned.1.call-start = ((), (), s32[]{:S(2)}) async-start(), calls=%async_computation.3 | async-start | bytes 4194304 | tf_op jit(solution)/shard_map/psum | solution.py:11
  436.7 1.7 copy-start.5
  544.4 170.4 %all-reduce.29.cloned.1.call-start = ((), (), s32[]{:S(2)}) async-start(), calls=%async_computation.4 | async-start | bytes 8388608 | tf_op jit(solution)/shard_map/psum | solution.py:11
  714.8 3.4 slice-start.2
  717.6 2.3 slice-start.3
  717.7 2.9 copy-start.3
Sparse Core Ops, SparseCore 0:
  18.1 59.2 all-reduce.20
  185.1 85.5 all-reduce.22
  275.2 80.1 all-reduce.30
  380.0 56.6 all-reduce.24
  544.5 85.5 all-reduce.26
  634.6 80.1 all-reduce.28
where the time goes:
time: 758 us; the launch traced here: 754 us
  waiting for transfers between devices  447 us (59%)
  other arithmetic  209 us (28%)
  matrix products  51.5 us (7%)
  local copies, waits for them, and re-layouts  30.7 us (4%)
  between operations  14.6 us (2%)
    psum x6, waiting for transfers between devices, from_root(): return lax.psum(block, axis)  447 us
    another operation x24, other arithmetic, factor_block(): lower = jnp.linalg.cholesky(block)  100 us
    another operation x16, other arithmetic, factor_block(): lax.linalg.triangular_solve(lower, eye, left_side=True, lower=True)  84.4 us
    dot_general x2, matrix products, apply_update(): jnp.einsum('arb,csb->arcs', row_panel, col_panel, precision=lax.Precision...  28.1 us
    dot_general x26, matrix products, mm(): return jnp.matmul(a, b, precision=HIGH)  21.2 us
  transfers between devices with their start and end apart: 6, of which 6 were waited for; matrix products, arithmetic and copies ran while one was open for 0% of the time, Pallas kernels for 0%

commit v1 on v0

--- a/solution.py
+++ b/solution.py
@@ -8,7 +8,7 @@
 
 def from_root(block, axis, source):
     block = jnp.where(lax.axis_index(axis) == source, block, jnp.zeros_like(block))
-    return lax.psum(block, axis)
+    return jnp.sum(lax.all_gather(block, axis), axis=0)
 
 
 def mm(a, b):

time: 758 us -> 1120 us (1.48)
  waiting for transfers between devices: 447 us -> 751 us
  other arithmetic: 209 us -> 262 us
  matrix products: 51.5 us -> 69.1 us
    all_gather x0 -> x8, waiting for transfers between devices: none -> 749 us  [from_root(): return jnp.sum(lax.all_gather(block, axis), axis=0)]
    psum x6 -> x0, waiting for transfers between devices: 447 us -> none  [from_root(): return lax.psum(block, axis)]
    reduce_sum x0 -> x8, other arithmetic: none -> 56 us  [from_root(): return jnp.sum(lax.all_gather(block, axis), axis=0)]
    dot_general x2, matrix products: 28.1 us -> 45.6 us  [apply_update(): jnp.einsum('arb,csb->arcs', row_panel, col_panel, precision=lax.Precision...]
  transfers between devices with their start and end apart: 6 -> 8, of which waited for: 6 -> 8; matrix products, arithmetic and copies ran while one was open for 0% -> 2% of each run, Pallas kernels for 0% -> 0%
where the time goes in v1:
time: 1120 us
  waiting for transfers between devices  751 us (67%)
  other arithmetic  262 us (23%)
  matrix products  69.1 us (6%)
  local copies, waits for them, and re-layouts  22.2 us (2%)
  between operations  14.5 us (1%)
    all_gather x8, waiting for transfers between devices, from_root(): return jnp.sum(lax.all_gather(block, axis), axis=0)  749 us
    another operation x24, other arithmetic, factor_block(): lower = jnp.linalg.cholesky(block)  101 us
    another operation x16, other arithmetic, factor_block(): lax.linalg.triangular_solve(lower, eye, left_side=True, lower=True)  84.1 us
    reduce_sum x8, other arithmetic, from_root(): return jnp.sum(lax.all_gather(block, axis), axis=0)  56 us
    dot_general x2, matrix products, apply_update(): jnp.einsum('arb,csb->arcs', row_panel, col_panel, precision=lax.Precision...  45.6 us
  transfers between devices with their start and end apart: 8, of which 8 were waited for; matrix products, arithmetic and copies ran while one was open for 2% of the time, Pallas kernels for 0%

profile of v1, /device:TPU:0, one launch (start us, length us, event | category | flops | bytes accessed | tf_op | source)
XLA Modules:
  0.0 1120.3 jit_solution(5132233927028684201)
XLA Ops:
  6.6 0.8 and_and_fusion
  7.4 6.6 bitcast_select_fusion
  14.1 3.4 copy-done
  17.5 1.2 fusion.18
  19.2 56.7 %all-gather.17.cloned.1.call-done = f32[8,512,1,512]{3,1,2,0:T(8,128)} async-done(((f32[1,512,1,512]{3,1,2,0:T(8,128)}), f32[8,512,1,512]{3,1,2,0:T(8,128)}) %all-gather.17.cloned.1.call-update) | async-done | bytes 8388624 | tf_op jit(solution)/shard_map/all_gather | solution.py:11
  75.9 4.5 reduce_sum.72
  81.1 11.7 %cholesky.134 = f32[128,128]{1,0:T(8,128)S(1)} custom-call(f32[128,128]{1,0:T(8,128)S(1)} %fusion.94), custom_call_target="Cholesky" | custom-call | tf_op jit(solution)/shard_map/jit(cholesky)/cholesky | solution.py:19
  92.9 0.7 compare_reduce_fusion.7
  94.3 9.8 custom-call.12
  105.3 11.9 %cholesky.145 = f32[128,128]{1,0:T(8,128)S(1)} custom-call(f32[128,128]{1,0:T(8,128)S(1)} %fusion.92), custom_call_target="Cholesky" | custom-call | tf_op jit(solution)/shard_map/jit(cholesky)/cholesky | solution.py:19
  118.6 9.8 custom-call.13
  130.3 11.7 %cholesky.156 = f32[128,128]{1,0:T(8,128)S(1)} custom-call(f32[128,128]{1,0:T(8,128)S(1)} %fusion.90), custom_call_target="Cholesky" | custom-call | tf_op jit(solution)/shard_map/jit(cholesky)/cholesky | solution.py:19
  143.5 9.8 custom-call.14
  155.4 12.1 %cholesky.167 = f32[128,128]{1,0:T(8,128)S(1)} custom-call(f32[128,128]{1,0:T(8,128)S(1)} %fusion.88), custom_call_target="Cholesky" | custom-call | tf_op jit(solution)/shard_map/jit(cholesky)/cholesky | solution.py:19
  169.0 9.8 custom-call.15
  180.0 6.6 select_select_fusion.1
  186.7 149.7 %all-gather.19.cloned.1.call-done = f32[8,512,512]{2,1,0:T(8,128)} async-done(((f32[2,512,512]{2,1,0:T(8,128)}), f32[8,512,512]{2,1,0:T(8,128)}) %all-gather.19.cloned.1.call-update) | async-done | bytes 8388624 | tf_op jit(solution)/shard_map/all_gather | solution.py:11
  336.4 4.7 reduce_sum.73
  341.1 2.8 broadcast_select_fusion.2
  344.9 87.2 %all-gather.23.cloned.1.call-done = f32[16,512,512]{2,1,0:T(8,128)} async-done(((f32[2,512,512]{2,1,0:T(8,128)}), f32[16,512,512]{2,1,0:T(8,128)}) %all-gather.23.cloned.1.call-update) | async-done | bytes 16777232 | tf_op jit(solution)/shard_map/all_gather | solution.py:11
  432.1 9.4 reduce_sum.75
  441.5 82.2 %all-gather.21.cloned.1.call-done = f32[16,512,512]{2,1,0:T(8,128)} async-done(((f32[2,512,512]{2,1,0:T(8,128)}), f32[16,512,512]{2,1,0:T(8,128)}) %all-gather.21.cloned.1.call-update) | async-done | bytes 16777232 | tf_op jit(solution)/shard_map/all_gather | solution.py:11
  523.7 9.4 reduce_sum.74
  533.2 2.7 pad_maximum_fusion
  535.8 22.3 %fusion = f32[2,512,4,512]{3,1,0,2:T(8,128)S(1)} fusion(f32[2,512,4,512]{3,1,0,2:T(8,128)} %copy-done, f32[2,512,512]{2,1,0:T(8,128)S(1)} %reduce_sum.73, pred[4]{0:T(512)(128)(4,1)S(1)} %get-tuple-element.32, pred[2,4]{0,1:T(4,128)(4,1)S(1)} %bitcast.183, f32[4,512,512,1]{2,1,3,0:T(8,128)S(1)} %bitcast.175), kind=kOutput, calls=%fused_computation.2 | convolution fusion | flops 12891193344 | bytes 23068684 | tf_op jit(solution)/shard_map/arb,csb->arcs/dot_general | solution.py:82
  558.2 3.4 copy-done.1
  561.6 1.2 fusion.12
  563.2 54.1 %all-gather.25.cloned.1.call-done = f32[8,512,1,512]{3,1,2,0:T(8,128)} async-done(((f32[1,512,1,512]{3,1,2,0:T(8,128)}), f32[8,512,1,512]{3,1,2,0:T(8,128)}) %all-gather.25.cloned.1.call-update) | async-done | bytes 8388624 | tf_op jit(solution)/shard_map/all_gather | solution.py:11
  617.3 4.5 reduce_sum.76
  622.5 11.7 %cholesky.178 = f32[128,128]{1,0:T(8,128)S(1)} custom-call(f32[128,128]{1,0:T(8,128)S(1)} %fusion.86), custom_call_target="Cholesky" | custom-call | tf_op jit(solution)/shard_map/jit(cholesky)/cholesky | solution.py:19
  635.7 9.8 custom-call.16
  646.7 11.9 %cholesky.189 = f32[128,128]{1,0:T(8,128)S(1)} custom-call(f32[128,128]{1,0:T(8,128)S(1)} %fusion.84), custom_call_target="Cholesky" | custom-call | tf_op jit(solution)/shard_map/jit(cholesky)/cholesky | solution.py:19
  660.0 9.8 custom-call.17
  671.7 11.7 %cholesky.200 = f32[128,128]{1,0:T(8,128)S(1)} custom-call(f32[128,128]{1,0:T(8,128)S(1)} %fusion.82), custom_call_target="Cholesky" | custom-call | tf_op jit(solution)/shard_map/jit(cholesky)/cholesky | solution.py:19
  684.9 9.8 custom-call.18
  696.8 12.1 %cholesky.211 = f32[128,128]{1,0:T(8,128)S(1)} custom-call(f32[128,128]{1,0:T(8,128)S(1)} %fusion.80), custom_call_target="Cholesky" | custom-call | tf_op jit(solution)/shard_map/jit(cholesky)/cholesky | solution.py:19
  710.4 9.8 custom-call.19
  721.4 6.6 select_select_fusion
  728.1 149.7 %all-gather.27.cloned.1.call-done = f32[8,512,512]{2,1,0:T(8,128)} async-done(((f32[2,512,512]{2,1,0:T(8,128)}), f32[8,512,512]{2,1,0:T(8,128)}) %all-gather.27.cloned.1.call-update) | async-done | bytes 8388624 | tf_op jit(solution)/shard_map/all_gather | solution.py:11
  877.8 4.7 reduce_sum.77
  882.5 2.8 broadcast_select_fusion
  886.1 87.4 %all-gather.31.cloned.1.call-done = f32[16,512,512]{2,1,0:T(8,128)} async-done(((f32[2,512,512]{2,1,0:T(8,128)}), f32[16,512,512]{2,1,0:T(8,128)}) %all-gather.31.cloned.1.call-update) | async-done | bytes 16777232 | tf_op jit(solution)/shard_map/all_gather | solution.py:11
  973.5 9.4 reduce_sum.79
  982.9 82.3 %all-gather.29.cloned.1.call-done = f32[16,512,512]{2,1,0:T(8,128)} async-done(((f32[2,512,512]{2,1,0:T(8,128)}), f32[16,512,512]{2,1,0:T(8,128)}) %all-gather.29.cloned.1.call-update) | async-done | bytes 16777232 | tf_op jit(solution)/shard_map/all_gather | solution.py:11
  1065.3 9.4 reduce_sum.78
  1074.7 2.7 pad_maximum_fusion.1
  1077.4 23.2 %fusion.2 = f32[2,1,512,4,1,512]{5,2,0,3,4,1:T(8,128)S(1)} fusion(f32[2,512,4,512]{3,1,0,2:T(8,128)} %copy-done.1, f32[2,512,512]{2,1,0:T(8,128)S(1)} %reduce_sum.77, pred[4]{0:T(512)(128)(4,1)S(1)} %broadcast_compare_fusion.7, pred[2,4]{0,1:T(4,128)(4,1)S(1)} %bitcast.184, f32[4,512,512,1]{2,1,3,0:T(8,128)S(1)} %bitcast.176), kind=kOutput, calls=%fused_computation.4 | convolution fusion | flops 12891193344 | bytes 23068684 | tf_op jit(solution)/shard_map/arb,csb->arcs/dot_general | solution.py:82
  1100.6 12.7 %copy.78 = f32[2,1,512,4,1,512]{5,4,3,2,1,0:T(1,128)} copy(f32[2,1,512,4,1,512]{5,2,0,3,4,1:T(8,128)S(1)} %fusion.2) | data formatting | bytes 16777216 | tf_op jit(solution)/shard_map/reshape | solution.py:91
  (127 shorter events, 27.7 us)
Async XLA Ops:
  6.5 69.4 %all-gather.17.cloned.1.call-start = ((), (), s32[]{:S(2)}) async-start(), calls=%async_computation | async-start | bytes 9437184 | tf_op jit(solution)/shard_map/all_gather | solution.py:11
  14.1 3.4 copy-start
  18.7 317.8 %all-gather.19.cloned.1.call-start = ((), (), s32[]{:S(2)}) async-start(), calls=%async_computation.1 | async-start | bytes 10485760 | tf_op jit(solution)/shard_map/all_gather | solution.py:11
  186.6 245.5 %all-gather.23.cloned.1.call-start = ((), (), s32[]{:S(2)}) async-start(), calls=%async_computation.3 | async-start | bytes 18874368 | tf_op jit(solution)/shard_map/all_gather | solution.py:11
  343.9 179.9 %all-gather.21.cloned.1.call-start = ((), (), s32[]{:S(2)}) async-start(), calls=%async_computation.2 | async-start | bytes 18874368 | tf_op jit(solution)/shard_map/all_gather | solution.py:11
  344.4 272.9 %all-gather.25.cloned.1.call-start = ((), (), s32[]{:S(2)}) async-start(), calls=%async_computation.4 | async-start | bytes 9437184 | tf_op jit(solution)/shard_map/all_gather | solution.py:11
  558.2 3.4 copy-start.1
  562.8 315.1 %all-gather.27.cloned.1.call-start = ((), (), s32[]{:S(2)}) async-start(), calls=%async_computation.5 | async-start | bytes 10485760 | tf_op jit(solution)/shard_map/all_gather | solution.py:11
  728.0 245.5 %all-gather.31.cloned.1.call-start = ((), (), s32[]{:S(2)}) async-start(), calls=%async_computation.7 | async-start | bytes 18874368 | tf_op jit(solution)/shard_map/all_gather | solution.py:11
  885.3 180.0 %all-gather.29.cloned.1.call-start = ((), (), s32[]{:S(2)}) async-start(), calls=%async_computation.6 | async-start | bytes 18874368 | tf_op jit(solution)/shard_map/all_gather | solution.py:11
Sparse Core Ops, SparseCore 0:
  18.8 57.0 all-gather.16
  186.7 149.6 all-gather.18
  344.0 88.0 all-gather.22
  433.8 89.8 all-gather.20
  562.9 54.3 all-gather.24
  728.1 149.6 all-gather.26
  885.4 88.0 all-gather.30
  975.4 89.8 all-gather.28
